TPU v7x, 32 devices: a whole 2x2x4 slice. The times are simulated.
32 devices in a mesh: gx: 4 (over z), gy: 4 (over y, x), gz: 2 (over core).
Axes of the slice: x: 2, y: 2, z: 4, core: 2. Of those that a mesh axis runs over, the one named last changes fastest.
Arguments:
- f_pop: float32 [19, 16, 64, 256], P(None, 'gx', 'gy', 'gz'), may hold values from 0.02 to 0.1
- g_pop: float32 [19, 16, 64, 256], P(None, 'gx', 'gy', 'gz'), may hold values from -0.2 to 0.2
- displacement: int32 [1], replicated, may hold values from 33 to 47
Outputs:
- f_new: float32 [19, 16, 64, 256], P(None, 'gx', 'gy', 'gz')
- g_new: float32 [19, 16, 64, 256], P(None, 'gx', 'gy', 'gz')
All inputs are finite; a program needn't handle non-finite values.
Results may differ from a plain program's by a relative error of at most 0.0001.
Values sent between devices are 32-bit elements; how exact they have to be, the bound alone decides.
A program may use at most 64 MiB of HBM per device.

v0:
```python
import jax
import jax.numpy as jnp
from jax import lax
from jax.sharding import PartitionSpec as P

VELOCITIES = [
    (0, 0, 0),
    (1, 0, 0),
    (1, 1, 0),
    (1, -1, 0),
    (1, 0, 1),
    (1, 0, -1),
    (-1, 0, 0),
    (-1, -1, 0),
    (-1, 1, 0),
    (-1, 0, -1),
    (-1, 0, 1),
    (0, 1, 0),
    (0, -1, 0),
    (0, 0, 1),
    (0, 0, -1),
    (0, 1, 1),
    (0, -1, -1),
    (0, 1, -1),
    (0, -1, 1),
]
BULK_COEF = 0.5
STIFFNESS = 0.5
TAU_FLUID = 0.8
TAU_ORDER = 0.9


def with_halo(cells, sides, width):
    for axis, dim in sides:
        count = lax.axis_size(axis)
        head = lax.slice_in_dim(cells, 0, width, axis=dim)
        tail = lax.slice_in_dim(cells, cells.shape[dim] - width, cells.shape[dim], axis=dim)
        cells = jnp.concatenate(
            [
                lax.ppermute(tail, axis, [(i, (i + 1) % count) for i in range(count)]),
                cells,
                lax.ppermute(head, axis, [((i + 1) % count, i) for i in range(count)]),
            ],
            axis=dim,
        )
    return cells


def lattice_weight(number):
    steps_sq = sum((abs(comp) for comp in VELOCITIES[number]))
    if steps_sq == 0:
        return 1.0 / 3.0
    if steps_sq == 1:
        return 1.0 / 18.0
    return 1.0 / 36.0


def along(number, values, base):
    result = jnp.zeros_like(base)
    for axis_id in range(3):
        comp = VELOCITIES[number][axis_id]
        if comp != 0:
            result = result + comp * values[axis_id]
    return result


def collide(f_pop, g_pop, order_field, laplace, slopes):
    density = jnp.sum(f_pop, axis=0)
    chemical = (
        BULK_COEF * (order_field * order_field * order_field - order_field) - STIFFNESS * laplace
    )
    forces = [chemical * slope for slope in slopes]
    moments = []
    for axis_id in range(3):
        moment = jnp.zeros_like(density)
        for number in range(19):
            comp = VELOCITIES[number][axis_id]
            if comp != 0:
                moment = moment + comp * f_pop[number]
        moments.append(moment)
    flows = [(moments[axis_id] + 0.5 * forces[axis_id]) / density for axis_id in range(3)]
    speed_sq = flows[0] * flows[0] + flows[1] * flows[1] + flows[2] * flows[2]
    flow_force = flows[0] * forces[0] + flows[1] * forces[1] + flows[2] * forces[2]
    f_posts = []
    g_eqs = []
    for number in range(19):
        weight = lattice_weight(number)
        proj_flow = along(number, flows, density)
        proj_force = along(number, forces, density)
        shape_term = 3.0 * proj_flow + 4.5 * proj_flow * proj_flow - 1.5 * speed_sq
        f_eq = weight * density * (1.0 + shape_term)
        source = (
            (1.0 - 0.5 / TAU_FLUID)
            * weight
            * (3.0 * (proj_force - flow_force) + 9.0 * proj_flow * proj_force)
        )
        f_posts.append(f_pop[number] - (f_pop[number] - f_eq) / TAU_FLUID + source)
        g_eqs.append(weight * (3.0 * chemical + order_field * shape_term))
    rest_eq = order_field
    for number in range(1, 19):
        rest_eq = rest_eq - g_eqs[number]
    g_eqs[0] = rest_eq
    g_posts = [g_pop[number] - (g_pop[number] - g_eqs[number]) / TAU_ORDER for number in range(19)]
    return (jnp.stack(f_posts), jnp.stack(g_posts))


def window(whole, begin, rows, whole_rows):
    begin = jnp.mod(begin, whole_rows)
    doubled = jnp.concatenate([whole, whole], axis=1)
    return lax.dynamic_slice_in_dim(doubled, begin, rows, 1)


def sliding(edges, shift):
    extended = with_halo(edges, (("gx", 1),), 1)
    below = extended[:, 0]
    above = extended[:, 3]
    whole_below, whole_above = (
        lax.all_gather(below, "gy", axis=1, tiled=True),
        lax.all_gather(above, "gy", axis=1, tiled=True),
    )
    rows = below.shape[1]
    whole_rows = whole_below.shape[1]
    start = lax.axis_index("gy") * rows
    return (
        window(whole_below, start - shift, rows, whole_rows),
        window(whole_above, start + shift, rows, whole_rows),
    )


def extend_x(posts, below, above):
    rows, layers = (posts.shape[2], posts.shape[3])
    lower = jnp.concatenate(
        [
            jnp.zeros((1, rows, layers), jnp.float32),
            below,
            jnp.zeros((13, rows, layers), jnp.float32),
        ],
        axis=0,
    )
    upper = jnp.concatenate(
        [
            jnp.zeros((6, rows, layers), jnp.float32),
            above,
            jnp.zeros((8, rows, layers), jnp.float32),
        ],
        axis=0,
    )
    return jnp.concatenate([lower[:, None], posts, upper[:, None]], axis=1)


def local(f_pop, g_pop, displacement):
    shift = displacement[0]
    width_x, width_y, width_z = (f_pop.shape[1], f_pop.shape[2], f_pop.shape[3])
    order_field = jnp.sum(g_pop, axis=0)
    phase_edges = jnp.stack([order_field[0], order_field[-1]])[None]
    phase_below, phase_above = sliding(phase_edges, shift)
    neigh_xm = jnp.concatenate([phase_below, order_field[:-1]], axis=0)
    neigh_xp = jnp.concatenate([order_field[1:], phase_above], axis=0)
    padded = with_halo(order_field, (("gy", 1), ("gz", 2)), 1)
    neigh_ym = padded[:, :-2, 1:-1]
    neigh_yp = padded[:, 2:, 1:-1]
    neigh_zm = padded[:, 1:-1, :-2]
    neigh_zp = padded[:, 1:-1, 2:]
    laplace = neigh_xm + neigh_xp + neigh_ym + neigh_yp + neigh_zm + neigh_zp - 6.0 * order_field
    slopes = [0.5 * (neigh_xp - neigh_xm), 0.5 * (neigh_yp - neigh_ym), 0.5 * (neigh_zp - neigh_zm)]
    f_post, g_post = collide(f_pop, g_pop, order_field, laplace, slopes)
    pop_edges = jnp.concatenate(
        [
            jnp.stack([f_post[6:11, 0], f_post[1:6, -1]], axis=1),
            jnp.stack([g_post[6:11, 0], g_post[1:6, -1]], axis=1),
        ],
        axis=0,
    )
    pop_below, pop_above = sliding(pop_edges, shift)
    layered = jnp.concatenate(
        [
            extend_x(f_post, pop_below[0:5], pop_above[0:5]),
            extend_x(g_post, pop_below[5:10], pop_above[5:10]),
        ],
        axis=0,
    )
    results = []
    padded_all = with_halo(layered, (("gy", 2), ("gz", 3)), 1)
    for number in range(38):
        vel_x, vel_y, vel_z = VELOCITIES[number % 19]
        results.append(
            padded_all[
                number,
                1 - vel_x : 1 - vel_x + width_x,
                1 - vel_y : 1 - vel_y + width_y,
                1 - vel_z : 1 - vel_z + width_z,
            ]
        )
    f_new = jnp.stack(results[:19])
    g_new = jnp.stack(results[19:])
    return (f_new, g_new)


def solution(mesh):
    return jax.shard_map(
        local,
        mesh=mesh,
        in_specs=(P(None, "gx", "gy", "gz"), P(None, "gx", "gy", "gz"), P()),
        out_specs=(P(None, "gx", "gy", "gz"), P(None, "gx", "gy", "gz")),
        check_vma=False,
    )
```

profile of v0, /device:TPU:0, one launch (start us, length us, event | category | flops | bytes accessed | tf_op | source)
XLA Modules:
  0.0 93.0 jit_solution(2654150964023462803)
XLA Ops:
  0.7 1.2 %reduce_sum.19 = f32[4,16,128]{2,1,0:T(8,128)S(1)} reduce(f32[19,4,16,128]{3,2,1,0:T(8,128)} %param.4, f32[]{:T(128)} %constant.95.clone.1), dimensions={0}, to_apply=%region_1.2 | reduce | flops 147456 | bytes 655364 | tf_op jit(solution)/shard_map/reduce_sum | solution.py:154
  1.9 3.9 %collective-permute-start.3 = (f32[4,1,128]{2,1,0:T(1,128)S(1)}, f32[4,1,128]{2,1,0:T(1,128)S(1)}, u32[]{:S(2)}, u32[]{:S(2)}) collective-permute-start(f32[4,1,128]{2,1,0:T(1,128)S(1)} %get-tuple-element.108), channel_id=1, source_target_pairs={{2,0},{4,2},{6,4},{0,6},{3,1},{5,3},{7,5},{1,7},{10,8},{12,10},{14... | collective-permute-start | bytes 6152 | tf_op jit(solution)/shard_map/ppermute | solution.py:42
  5.9 3.7 %collective-permute-start.1 = (f32[1,1,16,128]{3,2,1,0:T(8,128)S(1)}, f32[1,1,16,128]{3,2,1,0:T(8,128)S(1)}, u32[]{:S(2)}, u32[]{:S(2)}) collective-permute-start(f32[1,1,16,128]{3,2,1,0:T(8,128)S(1)} %get-tuple-element.114), channel_id=1, source_target_pairs={{8,0},{16,8},{24,16},{0,24},{9,1},{17,9},{25,17},{1,25},{10,2},{18... | collective-permute-start | bytes 24584 | tf_op jit(solution)/shard_map/ppermute | solution.py:42
  10.3 0.1 pad.67.clone
  10.3 0.1 pad.60.clone
  10.4 1.1 %reduce_sum.18 = f32[4,16,128]{2,1,0:T(8,128)S(1)} reduce(f32[19,4,16,128]{3,2,1,0:T(8,128)} %param.3, f32[]{:T(128)} %constant.95.clone.1), dimensions={0}, to_apply=%region_0.0 | reduce | flops 147456 | bytes 655364 | tf_op jit(solution)/shard_map/reduce_sum | solution.py:68
  11.6 0.1 fusion.109
  11.7 0.5 collective-permute-start.4
  12.2 2.8 %collective-permute-done = f32[1,1,16,128]{3,2,1,0:T(8,128)S(1)} collective-permute-done((f32[1,1,16,128]{3,2,1,0:T(8,128)S(1)}, f32[1,1,16,128]{3,2,1,0:T(8,128)S(1)}, u32[]{:S(2)}, u32[]{:S(2)}) %collective-permute-start) | collective-permute-done | bytes 8224 | tf_op jit(solution)/shard_map/ppermute | solution.py:40
  15.0 8.6 %all-gather = f32[1,1,64,128]{3,2,1,0:T(8,128)S(1)} all-gather(f32[1,1,16,128]{3,2,1,0:T(8,128)S(1)} %collective-permute-done), channel_id=2, replica_groups=mesh['gx'=4,'gy'=4,'gz'=2] {'gy'}, dimensions={2}, use_global_device_ids=true | all-gather | bytes 40960 | tf_op jit(solution)/shard_map/all_gather | solution.py:118
  23.6 8.2 %all-gather.1 = f32[1,1,64,128]{3,2,1,0:T(8,128)S(1)} all-gather(f32[1,1,16,128]{3,2,1,0:T(8,128)S(1)} %collective-permute-done.1), channel_id=3, replica_groups=mesh['gx'=4,'gy'=4,'gz'=2] {'gy'}, dimensions={2}, use_global_device_ids=true | all-gather | bytes 40960 | tf_op jit(solution)/shard_map/all_gather | solution.py:119
  31.8 1.4 %bitcast_subtract_fusion.16 = (f32[4,16,128]{2,1,0:T(8,128)S(1)}, f32[4,16,128]{2,1,0:T(8,128)S(1)}, f32[4,16,128]{2,1,0:T(8,128)S(1)}, f32[4,16,128]{2,1,0:T(8,...) fusion(f32[4,16,128]{2,1,0:T(8,128)S(1)} %reduce_sum.19, ...), kind=kLoop, calls=%fused_computation.190 | loop fusion | flops 2064384 | bytes 1512000 | tf_op jit(solution)/shard_map/sub | solution.py:103
  33.6 0.1 constant_dynamic-update-slice_fusion.3
  33.7 0.1 constant_dynamic-update-slice_fusion.2
  33.8 0.1 constant_dynamic-update-slice_fusion
  33.9 1.1 %collective-permute-start.7 = (f32[10,1,16,128]{3,2,1,0:T(8,128)S(1)}, f32[10,1,16,128]{3,2,1,0:T(8,128)S(1)}, u32[]{:S(2)}, u32[]{:S(2)}) collective-permute-start(f32[10,1,16,128]{3,2,1,0:T(8,128)S(1)} %get-tuple-element.92), channel_id=1, source_target_pairs={{8,0},{16,8},{24,16},{0,24},{9,1},{17,9},{25,17},{1,25},{10,2},{18... | collective-permute-start | bytes 245768 | tf_op jit(solution)/shard_map/ppermute | solution.py:42
  35.0 1.0 %collective-permute-start.6 = (f32[10,1,16,128]{3,2,1,0:T(8,128)S(1)}, f32[10,1,16,128]{3,2,1,0:T(8,128)S(1)}, u32[]{:S(2)}, u32[]{:S(2)}) collective-permute-start(f32[10,1,16,128]{3,2,1,0:T(8,128)S(1)} %get-tuple-element.93), channel_id=1, source_target_pairs={{0,8},{8,16},{16,24},{24,0},{1,9},{9,17},{17,25},{25,1},{2,10},{10... | collective-permute-start | bytes 245768 | tf_op jit(solution)/shard_map/ppermute | solution.py:40
  36.0 0.8 copy.371
  37.4 3.9 %collective-permute-done.6 = f32[10,1,16,128]{3,2,1,0:T(8,128)S(1)} collective-permute-done((f32[10,1,16,128]{3,2,1,0:T(8,128)S(1)}, f32[10,1,16,128]{3,2,1,0:T(8,128)S(1)}, u32[]{:S(2)}, u32[]{:S(2)}) %collective-permute-start.6) | collective-permute-done | bytes 81952 | tf_op jit(solution)/shard_map/ppermute | solution.py:40
  41.2 0.1 copy.282
  41.3 8.6 %all-gather.2 = f32[10,1,64,128]{3,1,0,2:T(1,128)S(1)} all-gather(f32[10,1,16,128]{3,1,0,2:T(1,128)S(1)} %copy.282), channel_id=4, replica_groups=mesh['gx'=4,'gy'=4,'gz'=2] {'gy'}, dimensions={2}, use_global_device_ids=true | all-gather | bytes 409600 | tf_op jit(solution)/shard_map/all_gather | solution.py:118
  50.0 0.1 copy.284
  50.1 10.7 %all-gather.3 = f32[10,1,64,128]{3,1,0,2:T(1,128)S(1)} all-gather(f32[10,1,16,128]{3,1,0,2:T(1,128)S(1)} %copy.284), channel_id=5, replica_groups=mesh['gx'=4,'gy'=4,'gz'=2] {'gy'}, dimensions={2}, use_global_device_ids=true | all-gather | bytes 409600 | tf_op jit(solution)/shard_map/all_gather | solution.py:119
  60.9 0.1 maximum_bitcast_fusion.2
  61.0 0.1 maximum_bitcast_fusion.1
  61.1 0.2 fusion
  61.3 0.1 collective-permute-start.8
  61.4 3.0 %collective-permute-start.9 = (f32[38,6,1,128]{3,0,2,1:T(8,128)S(1)}, f32[38,6,1,128]{3,0,2,1:T(8,128)S(1)}, u32[]{:S(2)}, u32[]{:S(2)}) collective-permute-start(f32[38,6,1,128]{3,0,2,1:T(8,128)S(1)} %copy.290), channel_id=1, source_target_pairs={{2,0},{4,2},{6,4},{0,6},{3,1},{5,3},{7,5},{1,7},{10,8},{12,10},{14... | collective-permute-start | bytes 350216 | tf_op jit(solution)/shard_map/ppermute | solution.py:42
  64.4 2.8 %collective-permute-done.8 = f32[38,6,1,128]{3,0,2,1:T(8,128)S(1)} collective-permute-done((f32[38,6,1,128]{3,0,2,1:T(8,128)S(1)}, f32[38,6,1,128]{3,0,2,1:T(8,128)S(1)}, u32[]{:S(2)}, u32[]{:S(2)}) %collective-permute-start.8) | collective-permute-done | bytes 116768 | tf_op jit(solution)/shard_map/ppermute | solution.py:40
  67.2 0.1 copy.289
  67.3 0.1 copy.291
  67.4 0.5 pad_maximum_fusion
  67.9 3.2 %fusion.105 = (f32[38,6,18,1]{3,2,1,0:T(8,128)}, f32[38,6,18,1]{3,2,1,0:T(8,128)}) fusion(f32[38,6,18,128]{3,2,1,0:T(8,128)S(1)} %pad_maximum_fusion), kind=kLoop, calls=%fused_computation.399 | loop fusion | bytes 65664 | tf_op jit(solution)/shard_map/slice | solution.py:36
  71.2 3.0 %copy.294 = f32[38,6,18,1]{0,2,3,1:T(8,128)S(1)} copy(f32[38,6,18,1]{3,2,1,0:T(8,128)} %get-tuple-element.53) | data formatting | bytes 32832 | tf_op jit(solution)/shard_map/slice | solution.py:37
  74.2 0.1 collective-permute-start.10
  74.3 3.0 %copy.296 = f32[38,6,18,1]{0,2,3,1:T(8,128)S(1)} copy(f32[38,6,18,1]{3,2,1,0:T(8,128)} %get-tuple-element.52) | data formatting | bytes 32832 | tf_op jit(solution)/shard_map/slice | solution.py:36
  77.3 0.5 collective-permute-start.11
  77.9 2.8 %copy.295 = f32[38,6,18,1]{3,2,1,0:T(8,128)} copy(f32[38,6,18,1]{0,2,3,1:T(8,128)S(1)} %collective-permute-done.10) | data formatting | bytes 32832 | tf_op jit(solution)/shard_map/ppermute | solution.py:40
  80.6 0.9 constant_dynamic-update-slice_fusion.91
  81.5 2.8 %copy.297 = f32[38,6,18,1]{3,2,1,0:T(8,128)} copy(f32[38,6,18,1]{0,2,3,1:T(8,128)S(1)} %collective-permute-done.11) | data formatting | bytes 32832 | tf_op jit(solution)/shard_map/ppermute | solution.py:42
  84.3 0.9 constant_dynamic-update-slice_fusion.90
  85.3 1.7 %copy-done.1 = f32[38,6,18,1]{3,2,1,0:T(8,128)S(1)} copy-done((f32[38,6,18,1]{3,2,1,0:T(8,128)S(1)}, f32[38,6,18,1]{3,2,1,0:T(8,128)}, u32[]{:S(2)}) %copy-start.1) | copy-done | bytes 16440
  87.0 0.1 constant_dynamic-update-slice_fusion.86
  87.1 1.7 %copy-done = f32[38,6,18,1]{3,2,1,0:T(8,128)S(1)} copy-done((f32[38,6,18,1]{3,2,1,0:T(8,128)S(1)}, f32[38,6,18,1]{3,2,1,0:T(8,128)}, u32[]{:S(2)}) %copy-start) | copy-done | bytes 16440
  88.8 0.1 constant_dynamic-update-slice_fusion.85
  88.9 0.1 constant_dynamic-update-slice_fusion.82
  89.0 0.1 constant_dynamic-update-slice_fusion.81
  89.1 1.0 %copy-done.5 = f32[19,4,16,128]{3,2,1,0:T(8,128)S(1)} copy-done((f32[19,4,16,128]{3,2,1,0:T(8,128)S(1)}, f32[19,4,16,128]{3,2,1,0:T(8,128)}, u32[]{:S(2)}) %copy-start.5) | copy-done | bytes 622616
  90.1 0.1 constant_dynamic-update-slice_fusion.80
  90.1 0.1 constant_dynamic-update-slice_fusion.79
  90.3 0.1 constant_dynamic-update-slice_fusion.72
  90.3 0.1 constant_dynamic-update-slice_fusion.71
  90.5 0.1 constant_dynamic-update-slice_fusion.78
  90.6 0.1 constant_dynamic-update-slice_fusion.67
  90.7 0.1 constant_dynamic-update-slice_fusion.66
  90.8 0.1 constant_dynamic-update-slice_fusion.77
  90.9 0.1 constant_dynamic-update-slice_fusion.63
  91.0 0.7 copy-done.4
  91.7 0.1 constant_dynamic-update-slice_fusion.62
  91.8 0.1 constant_dynamic-update-slice_fusion.61
  91.8 0.1 constant_dynamic-update-slice_fusion.60
  92.0 0.1 constant_dynamic-update-slice_fusion.59
  92.1 0.1 constant_dynamic-update-slice_fusion.58
  92.2 0.8 copy-done.6
  (97 shorter events, 1.2 us)
Async XLA Ops:
  0.6 32.7 %copy-start.3 = (f32[19,4,16,128]{3,2,1,0:T(8,128)S(1)}, f32[19,4,16,128]{3,2,1,0:T(8,128)}, u32[]{:S(2)}) copy-start(f32[19,4,16,128]{3,2,1,0:T(8,128)} %param.4) | copy-start | bytes 1867780
  0.6 32.6 %copy-start.2 = (f32[19,4,16,128]{3,2,1,0:T(8,128)S(1)}, f32[19,4,16,128]{3,2,1,0:T(8,128)}, u32[]{:S(2)}) copy-start(f32[19,4,16,128]{3,2,1,0:T(8,128)} %param.3) | copy-start | bytes 1867780
  1.9 9.7 %collective-permute-start.3 = (f32[4,1,128]{2,1,0:T(1,128)S(1)}, f32[4,1,128]{2,1,0:T(1,128)S(1)}, u32[]{:S(2)}, u32[]{:S(2)}) collective-permute-start(f32[4,1,128]{2,1,0:T(1,128)S(1)} %get-tuple-element.108), channel_id=1, source_target_pairs={{2,0},{4,2},{6,4},{0,6},{3,1},{5,3},{7,5},{1,7},{10,8},{12,10},{14... | collective-permute-start | bytes 6152 | tf_op jit(solution)/shard_map/ppermute | solution.py:42
  5.8 5.7 %collective-permute-start.2 = (f32[4,1,128]{2,1,0:T(1,128)S(1)}, f32[4,1,128]{2,1,0:T(1,128)S(1)}, u32[]{:S(2)}, u32[]{:S(2)}) collective-permute-start(f32[4,1,128]{2,1,0:T(1,128)S(1)} %get-tuple-element.109), channel_id=1, source_target_pairs={{0,2},{2,4},{4,6},{6,0},{1,3},{3,5},{5,7},{7,1},{8,10},{10,12},{12... | collective-permute-start | bytes 6152 | tf_op jit(solution)/shard_map/ppermute | solution.py:40
  5.9 17.7 %collective-permute-start.1 = (f32[1,1,16,128]{3,2,1,0:T(8,128)S(1)}, f32[1,1,16,128]{3,2,1,0:T(8,128)S(1)}, u32[]{:S(2)}, u32[]{:S(2)}) collective-permute-start(f32[1,1,16,128]{3,2,1,0:T(8,128)S(1)} %get-tuple-element.114), channel_id=1, source_target_pairs={{8,0},{16,8},{24,16},{0,24},{9,1},{17,9},{25,17},{1,25},{10,2},{18... | collective-permute-start | bytes 24584 | tf_op jit(solution)/shard_map/ppermute | solution.py:42
  9.5 5.4 %collective-permute-start = (f32[1,1,16,128]{3,2,1,0:T(8,128)S(1)}, f32[1,1,16,128]{3,2,1,0:T(8,128)S(1)}, u32[]{:S(2)}, u32[]{:S(2)}) collective-permute-start(f32[1,1,16,128]{3,2,1,0:T(8,128)S(1)} %get-tuple-element.115), channel_id=1, source_target_pairs={{0,8},{8,16},{16,24},{24,0},{1,9},{9,17},{17,25},{25,1},{2,10},{10... | collective-permute-start | bytes 24584 | tf_op jit(solution)/shard_map/ppermute | solution.py:40
  11.7 20.1 %collective-permute-start.5 = (f32[4,18,1]{2,1,0:T(8,128)S(1)}, f32[4,18,1]{2,1,0:T(8,128)S(1)}, u32[]{:S(2)}, u32[]{:S(2)}) collective-permute-start(f32[4,18,1]{2,1,0:T(8,128)S(1)} %get-tuple-element.106), channel_id=1, source_target_pairs={{1,0},{0,1},{3,2},{2,3},{5,4},{4,5},{7,6},{6,7},{9,8},{8,9},{11,10... | collective-permute-start | bytes 872 | tf_op jit(solution)/shard_map/ppermute | solution.py:42
  11.7 20.1 %collective-permute-start.4 = (f32[4,18,1]{2,1,0:T(8,128)S(1)}, f32[4,18,1]{2,1,0:T(8,128)S(1)}, u32[]{:S(2)}, u32[]{:S(2)}) collective-permute-start(f32[4,18,1]{2,1,0:T(8,128)S(1)} %get-tuple-element.107), channel_id=1, source_target_pairs={{0,1},{1,0},{2,3},{3,2},{4,5},{5,4},{6,7},{7,6},{8,9},{9,8},{10,11... | collective-permute-start | bytes 872 | tf_op jit(solution)/shard_map/ppermute | solution.py:40
  33.9 16.1 %collective-permute-start.7 = (f32[10,1,16,128]{3,2,1,0:T(8,128)S(1)}, f32[10,1,16,128]{3,2,1,0:T(8,128)S(1)}, u32[]{:S(2)}, u32[]{:S(2)}) collective-permute-start(f32[10,1,16,128]{3,2,1,0:T(8,128)S(1)} %get-tuple-element.92), channel_id=1, source_target_pairs={{8,0},{16,8},{24,16},{0,24},{9,1},{17,9},{25,17},{1,25},{10,2},{18... | collective-permute-start | bytes 245768 | tf_op jit(solution)/shard_map/ppermute | solution.py:42
  35.0 6.2 %collective-permute-start.6 = (f32[10,1,16,128]{3,2,1,0:T(8,128)S(1)}, f32[10,1,16,128]{3,2,1,0:T(8,128)S(1)}, u32[]{:S(2)}, u32[]{:S(2)}) collective-permute-start(f32[10,1,16,128]{3,2,1,0:T(8,128)S(1)} %get-tuple-element.93), channel_id=1, source_target_pairs={{0,8},{8,16},{16,24},{24,0},{1,9},{9,17},{17,25},{25,1},{2,10},{10... | collective-permute-start | bytes 245768 | tf_op jit(solution)/shard_map/ppermute | solution.py:40
  61.3 5.8 %collective-permute-start.8 = (f32[38,6,1,128]{3,0,2,1:T(8,128)S(1)}, f32[38,6,1,128]{3,0,2,1:T(8,128)S(1)}, u32[]{:S(2)}, u32[]{:S(2)}) collective-permute-start(f32[38,6,1,128]{3,0,2,1:T(8,128)S(1)} %copy.288), channel_id=1, source_target_pairs={{0,2},{2,4},{4,6},{6,0},{1,3},{3,5},{5,7},{7,1},{8,10},{10,12},{12... | collective-permute-start | bytes 350216 | tf_op jit(solution)/shard_map/ppermute | solution.py:40
  61.4 5.9 %collective-permute-start.9 = (f32[38,6,1,128]{3,0,2,1:T(8,128)S(1)}, f32[38,6,1,128]{3,0,2,1:T(8,128)S(1)}, u32[]{:S(2)}, u32[]{:S(2)}) collective-permute-start(f32[38,6,1,128]{3,0,2,1:T(8,128)S(1)} %copy.290), channel_id=1, source_target_pairs={{2,0},{4,2},{6,4},{0,6},{3,1},{5,3},{7,5},{1,7},{10,8},{12,10},{14... | collective-permute-start | bytes 350216 | tf_op jit(solution)/shard_map/ppermute | solution.py:42
  74.2 3.7 %collective-permute-start.10 = (f32[38,6,18,1]{0,2,3,1:T(8,128)S(1)}, f32[38,6,18,1]{0,2,3,1:T(8,128)S(1)}, u32[]{:S(2)}, u32[]{:S(2)}) collective-permute-start(f32[38,6,18,1]{0,2,3,1:T(8,128)S(1)} %copy.294), channel_id=1, source_target_pairs={{0,1},{1,0},{2,3},{3,2},{4,5},{5,4},{6,7},{7,6},{8,9},{9,8},{10,11... | collective-permute-start | bytes 49256 | tf_op jit(solution)/shard_map/ppermute | solution.py:40
  77.3 4.2 %collective-permute-start.11 = (f32[38,6,18,1]{0,2,3,1:T(8,128)S(1)}, f32[38,6,18,1]{0,2,3,1:T(8,128)S(1)}, u32[]{:S(2)}, u32[]{:S(2)}) collective-permute-start(f32[38,6,18,1]{0,2,3,1:T(8,128)S(1)} %copy.296), channel_id=1, source_target_pairs={{1,0},{0,1},{3,2},{2,3},{5,4},{4,5},{7,6},{6,7},{9,8},{8,9},{11,10... | collective-permute-start | bytes 49256 | tf_op jit(solution)/shard_map/ppermute | solution.py:42
  85.2 1.8 %copy-start.1 = (f32[38,6,18,1]{3,2,1,0:T(8,128)S(1)}, f32[38,6,18,1]{3,2,1,0:T(8,128)}, u32[]{:S(2)}) copy-start(f32[38,6,18,1]{3,2,1,0:T(8,128)} %copy.297) | copy-start | bytes 49252
  87.0 1.8 %copy-start = (f32[38,6,18,1]{3,2,1,0:T(8,128)S(1)}, f32[38,6,18,1]{3,2,1,0:T(8,128)}, u32[]{:S(2)}) copy-start(f32[38,6,18,1]{3,2,1,0:T(8,128)} %copy.295) | copy-start | bytes 49252
  89.0 1.1 %copy-start.5 = (f32[19,4,16,128]{3,2,1,0:T(8,128)S(1)}, f32[19,4,16,128]{3,2,1,0:T(8,128)}, u32[]{:S(2)}) copy-start(f32[19,4,16,128]{3,2,1,0:T(8,128)} %copy.371) | copy-start | bytes 1867780
  90.8 0.8 copy-start.4
  92.1 0.8 copy-start.6
where the time goes:
time: 93.6 us; the launch traced here: 93 us
  blocking collectives  36 us (38%)
  local copies, waits for them, and re-layouts  22.6 us (24%)
  starting transfers between devices  13.8 us (15%)
  waiting for transfers between devices  9.47 us (10%)
  other arithmetic  8.9 us (10%)
  between operations  2.17 us (2%)
    all_gather x2, blocking collectives, sliding(): lax.all_gather(above, 'gy', axis=1, tiled=True)  18.9 us
    all_gather x2, blocking collectives, sliding(): lax.all_gather(below, 'gy', axis=1, tiled=True)  17.2 us
    ppermute x6, starting transfers between devices, with_halo(): lax.ppermute(head, axis, [((i + 1) % count, i) for i in range(count)])  12.2 us
    ppermute x6, waiting for transfers between devices, with_halo(): lax.ppermute(tail, axis, [(i, (i + 1) % count) for i in range(count)])  9.46 us
    unnamed x27, local copies, waits for them, and re-layouts  6.9 us
    slice x7, local copies, waits for them, and re-layouts, with_halo(): head = lax.slice_in_dim(cells, 0, width, axis=dim)  6.39 us
    unnamed x56, other arithmetic  3.93 us
    slice x2, local copies, waits for them, and re-layouts, with_halo(): lax.slice_in_dim(cells, cells.shape[dim] - width, cells.shape[dim], axis=...  3.05 us
  transfers between devices with their start and end apart: 12, of which 3 were waited for; matrix products, arithmetic and copies ran while one was open for 10% of the time, Pallas kernels for 0%

commit v1 on v0

v1 whole, which is shorter than its diff:
```python
import functools

import jax
import jax.numpy as jnp
from jax import lax
from jax.experimental import pallas as pl
from jax.experimental.pallas import tpu as pltpu
from jax.sharding import PartitionSpec as P

VELOCITIES = [
    (0, 0, 0),
    (1, 0, 0),
    (1, 1, 0),
    (1, -1, 0),
    (1, 0, 1),
    (1, 0, -1),
    (-1, 0, 0),
    (-1, -1, 0),
    (-1, 1, 0),
    (-1, 0, -1),
    (-1, 0, 1),
    (0, 1, 0),
    (0, -1, 0),
    (0, 0, 1),
    (0, 0, -1),
    (0, 1, 1),
    (0, -1, -1),
    (0, 1, -1),
    (0, -1, 1),
]
POPS = 19
TAU_FLUID = 0.8
TAU_ORDER = 0.9
PAIRS = [(1, 6), (2, 7), (3, 8), (4, 9), (5, 10), (11, 12), (13, 14), (15, 16), (17, 18)]
Z_PAIRS = [(4, 5), (10, 9), (13, 14), (15, 16), (18, 17)]
Y_UP = [2, 8, 11, 15, 17]
Y_DOWN = [3, 7, 12, 16, 18]
UP = [(0, 1), (0, 2), (0, 3), (1, 1), (1, 2), (1, 3), (0, 4), (0, 5), (1, 4), (1, 5)]
DOWN = [(0, 6), (0, 7), (0, 8), (1, 6), (1, 7), (1, 8), (0, 9), (0, 10), (1, 9), (1, 10)]
FIRST = 6
MESH = pl.DeviceIdType.MESH


def kernel(
    sizes,
    shift_ref,
    f_hbm,
    g_hbm,
    f_out,
    g_out,
    f_ref,
    g_ref,
    phi_ref,
    phi_z,
    phi_ys,
    phi_yr,
    phi_lo,
    phi_hi,
    q_ref,
    z_send,
    z_recv,
    up_send,
    down_send,
    lo_one,
    lo_two,
    hi_one,
    hi_two,
    y_send,
    y_recv,
    local_sem,
    send_sem,
    recv_sem,
):
    count_x, count_y, count_z = sizes
    planes, rows, lanes = f_ref.shape[1:]
    a, b, c = lax.axis_index("gx"), lax.axis_index("gy"), lax.axis_index("gz")
    half = count_y // 2

    def at(dx, dy, dz=0):
        return (
            lax.rem(a + dx + count_x, count_x),
            lax.rem(b + dy + count_y, count_y),
            lax.rem(c + dz, count_z),
        )

    next_near, next_far = at(1, half), at(1, half + 1)
    prev_near, prev_far = at(-1, -half), at(-1, -half - 1)
    y_next, y_prev, z_other = at(0, 1), at(0, -1), at(0, 0, 1)

    load_g = pltpu.make_async_copy(g_hbm, g_ref, local_sem.at[0])
    load_f = pltpu.make_async_copy(f_hbm, f_ref, local_sem.at[1])
    load_g.start()
    load_f.start()
    barrier = pltpu.get_barrier_semaphore()
    partners = (next_near, next_far, prev_near, prev_far, y_next, y_prev, z_other)
    for partner in partners:
        pl.semaphore_signal(barrier, inc=1, device_id=partner, device_id_type=MESH)

    used = [0]

    def send(src, dst, target):
        slot = used[0]
        used[0] += 1
        copy = pltpu.make_async_remote_copy(
            src_ref=src,
            dst_ref=dst,
            send_sem=send_sem.at[slot],
            recv_sem=recv_sem.at[slot],
            device_id=target,
            device_id_type=MESH,
        )
        copy.start()
        return copy

    load_g.wait()
    for x in range(planes):
        parts = [g_ref[i, x] for i in range(POPS)]
        while len(parts) > 1:
            parts = [
                parts[k] + parts[k + 1] if k + 1 < len(parts) else parts[k]
                for k in range(0, len(parts), 2)
            ]
        phi_ref[x + 1] = parts[0]
        phi_ys[0, x : x + 1, :] = parts[0][rows - 1 : rows]
        phi_ys[1, x : x + 1, :] = parts[0][0:1]
    pl.semaphore_wait(barrier, len(partners))

    low, high = pl.ds(0, rows), pl.ds(rows, rows)
    last = planes
    slides = [
        send(phi_ref.at[last], phi_lo.at[low], next_far),
        send(phi_ref.at[last], phi_lo.at[high], next_near),
        send(phi_ref.at[1], phi_hi.at[low], prev_near),
        send(phi_ref.at[1], phi_hi.at[high], prev_far),
    ]
    to_z = send(phi_ref.at[pl.ds(1, planes)], phi_z, z_other)
    to_up = send(phi_ys.at[0], phi_yr.at[0], y_next)
    to_down = send(phi_ys.at[1], phi_yr.at[1], y_prev)

    lane = lax.broadcasted_iota(jnp.int32, (rows, lanes), 1)
    row = lax.broadcasted_iota(jnp.int32, (rows, lanes), 0)
    lane_first, lane_last = lane == 0, lane == lanes - 1
    row_first, row_last = row == 0, row == rows - 1
    residue = jnp.clip(shift_ref[0] - half * rows, 1, rows - 1)

    def collide(x, put):
        phi = phi_ref[x + 1]
        xm, xp = phi_ref[x], phi_ref[x + 2]
        ym = jnp.where(row_first, phi_yr[0, pl.ds(x, 1), :], pltpu.roll(phi, 1, 0))
        yp = jnp.where(row_last, phi_yr[1, pl.ds(x, 1), :], pltpu.roll(phi, rows - 1, 0))
        other = phi_z[x]
        zm = pltpu.roll(jnp.where(lane_last, other, phi), 1, 1)
        zp = pltpu.roll(jnp.where(lane_first, other, phi), lanes - 1, 1)
        laplace = xm + xp + ym + yp + zm + zp - 6.0 * phi
        chemical = 0.5 * (phi * phi * phi - phi) - 0.5 * laplace
        half_mu = 0.5 * chemical
        force = [half_mu * (xp - xm), half_mu * (yp - ym), half_mu * (zp - zm)]
        f = [f_ref[i, x] for i in range(POPS)]
        even_sum = f[0]
        moment = [None, None, None]
        for plus, minus in PAIRS:
            even_sum = even_sum + (f[plus] + f[minus])
            diff = f[plus] - f[minus]
            for axis in range(3):
                comp = VELOCITIES[plus][axis]
                if comp:
                    if moment[axis] is None:
                        moment[axis] = diff
                    elif comp > 0:
                        moment[axis] = moment[axis] + diff
                    else:
                        moment[axis] = moment[axis] - diff
        density = even_sum
        inverse = 1.0 / density
        flow = [(moment[axis] + 0.5 * force[axis]) * inverse for axis in range(3)]
        usq = flow[0] * flow[0] + flow[1] * flow[1] + flow[2] * flow[2]
        flow_force = flow[0] * force[0] + flow[1] * force[1] + flow[2] * force[2]

        inv_f, inv_g = 1.0 / TAU_FLUID, 1.0 / TAU_ORDER
        keep_f, keep_g = 1.0 - inv_f, 1.0 - inv_g
        gain = 1.0 - 0.5 / TAU_FLUID
        f_base = inv_f * density * (1.0 - 1.5 * usq) - (3.0 * gain) * flow_force
        f_square = (4.5 * inv_f) * density
        f_line = (3.0 * inv_f) * density
        g_base = inv_g * (3.0 * chemical - 1.5 * phi * usq)
        g_square = (4.5 * inv_g) * phi
        g_line = (3.0 * inv_g) * phi
        put(0, 0, keep_f * f[0] + (1.0 / 3.0) * f_base)
        put(1, 0, keep_g * g_ref[0, x] + inv_g * (phi - 2.0 * chemical - 0.5 * phi * usq))

        def dot(number, values):
            total = None
            for axis in range(3):
                comp = VELOCITIES[number][axis]
                if comp:
                    if total is None:
                        total = values[axis] if comp > 0 else -values[axis]
                    else:
                        total = total + values[axis] if comp > 0 else total - values[axis]
            return total

        done = {}
        for plus, minus in PAIRS:
            weight = 1.0 / 18.0 if sum(abs(v) for v in VELOCITIES[plus]) == 1 else 1.0 / 36.0
            cu = dot(plus, flow)
            cf = dot(plus, force)
            f_even = weight * (f_base + cu * (f_square * cu + (9.0 * gain) * cf))
            f_odd = weight * (f_line * cu + (3.0 * gain) * cf)
            g_even = weight * (g_base + g_square * (cu * cu))
            g_odd = weight * (g_line * cu)
            done[0, plus] = keep_f * f[plus] + (f_even + f_odd)
            done[0, minus] = keep_f * f[minus] + (f_even - f_odd)
            done[1, plus] = keep_g * g_ref[plus, x] + (g_even + g_odd)
            done[1, minus] = keep_g * g_ref[minus, x] + (g_even - g_odd)
        for (field, number), value in done.items():
            put(field, number, value)
        for field in range(2):
            for k, (plus, minus) in enumerate(Z_PAIRS):
                z_send[x, field * 5 + k] = jnp.where(
                    lane_last, done[field, plus], done[field, minus]
                )

    to_z.wait_recv()
    to_up.wait_recv()
    to_down.wait_recv()
    load_f.wait()

    def inner(x, carry):
        def put(field, number, value):
            q_ref[field * POPS + number, x + VELOCITIES[number][0]] = value

        collide(x, put)
        return carry

    lax.fori_loop(1, planes - 1, inner, 0)
    middle = pl.ds(1, planes - 2)
    z_mid = send(z_send.at[middle], z_recv.at[middle], z_other)

    def put_top(field, number, value):
        if VELOCITIES[number][0] == 1:
            up_send[UP.index((field, number))] = value
        else:
            q_ref[field * POPS + number, planes - 1 + VELOCITIES[number][0]] = value

    def put_bottom(field, number, value):
        if VELOCITIES[number][0] == -1:
            down_send[DOWN.index((field, number))] = value
        else:
            q_ref[field * POPS + number, VELOCITIES[number][0]] = value

    for copy in slides:
        copy.wait()
    start_lo, start_hi = rows - residue, residue
    phi_ref[0] = phi_lo[pl.ds(start_lo, rows), :]
    phi_ref[planes + 1] = phi_hi[pl.ds(start_hi, rows), :]

    part_one, part_two = pl.ds(0, FIRST), pl.ds(FIRST, len(UP) - FIRST)

    def send_up(part, recv):
        return [
            send(up_send.at[part], recv.at[:, high], next_near),
            send(up_send.at[part], recv.at[:, low], next_far),
        ]

    def send_down(part, recv):
        return [
            send(down_send.at[part], recv.at[:, low], prev_near),
            send(down_send.at[part], recv.at[:, high], prev_far),
        ]

    collide(planes - 1, put_top)
    first_up = send_up(part_one, lo_one)
    z_top = send(z_send.at[planes - 1], z_recv.at[planes - 1], z_other)
    collide(0, put_bottom)
    first_down = send_down(part_one, hi_one)
    z_bottom = send(z_send.at[0], z_recv.at[0], z_other)

    def along_z(x, k, field, number, value):
        plane = z_recv[x, field * 5 + k]
        if VELOCITIES[number][2] == 1:
            return pltpu.roll(jnp.where(lane_last, plane, value), 1, 1)
        return pltpu.roll(jnp.where(lane_first, plane, value), lanes - 1, 1)

    z_top.wait_recv()
    for field in range(2):
        for number in (4, 5):
            slot = UP.index((field, number))
            up_send[slot] = along_z(planes - 1, 0, field, number, up_send[slot])
    second_up = send_up(part_two, lo_two)
    z_bottom.wait_recv()
    for field in range(2):
        for number in (9, 10):
            slot = DOWN.index((field, number))
            down_send[slot] = along_z(0, 1, field, number, down_send[slot])
    second_down = send_down(part_two, hi_two)
    z_mid.wait_recv()

    for field in range(2):
        for k, pair in enumerate(Z_PAIRS):
            for number in pair:
                step = VELOCITIES[number][0]
                for x in range(max(0, -step), planes - max(0, step)):
                    index = field * POPS + number
                    q_ref[index, x + step] = along_z(x, k, field, number, q_ref[index, x + step])

    def stays(number):
        step = VELOCITIES[number][0]
        return range(max(0, step), planes + min(0, step))

    for field in range(2):
        for k in range(5):
            for side, numbers, edge in ((0, Y_UP, rows - 1), (1, Y_DOWN, 0)):
                for x in stays(numbers[k]):
                    spot = (field * 5 + k) * planes + x
                    y_send[side, spot : spot + 1, :] = q_ref[
                        field * POPS + numbers[k], x, edge : edge + 1, :
                    ]
    y_up = send(y_send.at[0], y_recv.at[0], y_next)
    y_down = send(y_send.at[1], y_recv.at[1], y_prev)
    y_up.wait_recv()
    y_down.wait_recv()
    for field in range(2):
        for k in range(5):
            for x in stays(Y_UP[k]):
                spot = (field * 5 + k) * planes + x
                index = field * POPS + Y_UP[k]
                q_ref[index, x] = jnp.where(
                    row_first, y_recv[0, spot : spot + 1, :], pltpu.roll(q_ref[index, x], 1, 0)
                )
            for x in stays(Y_DOWN[k]):
                spot = (field * 5 + k) * planes + x
                index = field * POPS + Y_DOWN[k]
                q_ref[index, x] = jnp.where(
                    row_last,
                    y_recv[1, spot : spot + 1, :],
                    pltpu.roll(q_ref[index, x], rows - 1, 0),
                )

    stores = []

    def store(field, pops, span):
        out = (f_out, g_out)[field]
        lo, hi = pops
        copy = pltpu.make_async_copy(
            q_ref.at[pl.ds(field * POPS + lo, hi - lo), span],
            out.at[pl.ds(lo, hi - lo), span],
            local_sem.at[2 + len(stores)],
        )
        copy.start()
        stores.append(copy)

    for field in range(2):
        store(field, (0, 1), pl.ds(0, planes))
        store(field, (1, 6), pl.ds(1, planes - 1))
        store(field, (6, 11), pl.ds(0, planes - 1))
        store(field, (11, POPS), pl.ds(0, planes))

    def land(offset, lo_recv, hi_recv):
        for slot in range(lo_recv.shape[0]):
            field, number = UP[offset + slot]
            begin = start_lo - VELOCITIES[number][1]
            q_ref[field * POPS + number, 0] = lo_recv[slot, pl.ds(begin, rows), :]
            field, number = DOWN[offset + slot]
            begin = start_hi - VELOCITIES[number][1]
            q_ref[field * POPS + number, planes - 1] = hi_recv[slot, pl.ds(begin, rows), :]

    for copy in first_up + first_down:
        copy.wait()
    land(0, lo_one, hi_one)
    for copy in second_up + second_down:
        copy.wait()
    land(FIRST, lo_two, hi_two)
    for field in range(2):
        store(field, (1, 6), pl.ds(0, 1))
        store(field, (6, 11), pl.ds(planes - 1, 1))
    for copy in (to_z, to_up, to_down, z_mid, z_top, z_bottom, y_up, y_down):
        copy.wait_send()
    for copy in stores:
        copy.wait()


def local(sizes, f_pop, g_pop, displacement):
    planes, rows, lanes = f_pop.shape[1:]
    block = (rows, lanes)
    f32 = jnp.float32
    crossing = len(UP)
    copies = 20
    return pl.pallas_call(
        functools.partial(kernel, sizes),
        out_shape=(
            jax.ShapeDtypeStruct(f_pop.shape, f32),
            jax.ShapeDtypeStruct(g_pop.shape, f32),
        ),
        in_specs=[
            pl.BlockSpec(memory_space=pltpu.SMEM),
            pl.BlockSpec(memory_space=pl.ANY),
            pl.BlockSpec(memory_space=pl.ANY),
        ],
        out_specs=[pl.BlockSpec(memory_space=pl.ANY)] * 2,
        scratch_shapes=[
            pltpu.VMEM(f_pop.shape, f32),
            pltpu.VMEM(g_pop.shape, f32),
            pltpu.VMEM((planes + 2,) + block, f32),
            pltpu.VMEM((planes,) + block, f32),
            pltpu.VMEM((2, planes, lanes), f32),
            pltpu.VMEM((2, planes, lanes), f32),
            pltpu.VMEM((2 * rows, lanes), f32),
            pltpu.VMEM((2 * rows, lanes), f32),
            pltpu.VMEM((2 * POPS, planes) + block, f32),
            pltpu.VMEM((planes, 10) + block, f32),
            pltpu.VMEM((planes, 10) + block, f32),
            pltpu.VMEM((crossing,) + block, f32),
            pltpu.VMEM((crossing,) + block, f32),
            pltpu.VMEM((FIRST, 2 * rows, lanes), f32),
            pltpu.VMEM((crossing - FIRST, 2 * rows, lanes), f32),
            pltpu.VMEM((FIRST, 2 * rows, lanes), f32),
            pltpu.VMEM((crossing - FIRST, 2 * rows, lanes), f32),
            pltpu.VMEM((2, 10 * planes, lanes), f32),
            pltpu.VMEM((2, 10 * planes, lanes), f32),
            pltpu.SemaphoreType.DMA((14,)),
            pltpu.SemaphoreType.DMA((copies,)),
            pltpu.SemaphoreType.DMA((copies,)),
        ],
        compiler_params=pltpu.CompilerParams(
            collective_id=0, has_side_effects=True, vmem_limit_bytes=24 * 1024 * 1024
        ),
    )(displacement, f_pop, g_pop)


def solution(mesh):
    sizes = tuple(mesh.shape[axis] for axis in ("gx", "gy", "gz"))
    return jax.shard_map(
        functools.partial(local, sizes),
        mesh=mesh,
        in_specs=(P(None, "gx", "gy", "gz"), P(None, "gx", "gy", "gz"), P()),
        out_specs=(P(None, "gx", "gy", "gz"), P(None, "gx", "gy", "gz")),
        check_vma=False,
    )
```

time: 93.6 us -> 25.5 us (0.27)
  blocking collectives: 36 us -> 0 us
  Pallas kernels: 0 us -> 20.2 us
  local copies, waits for them, and re-layouts: 22.6 us -> 3.8 us
  starting transfers between devices: 13.8 us -> 0 us
  waiting for transfers between devices: 9.47 us -> 0 us
  other arithmetic: 8.9 us -> 0 us
    all_gather x4 -> x0, blocking collectives: 36 us -> none  [the longest x2 18.9 us: sliding(): lax.all_gather(above, 'gy', axis=1, tiled=True)]
    pallas_call x0 -> x1, Pallas kernels: none -> 20.2 us  [local(): pl.pallas_call(functools.partial(kernel, sizes), out_shape=(jax.ShapeDtyp...]
    ppermute x12 -> x0, starting transfers between devices: 13.8 us -> none  [the longest x6 12.2 us: with_halo(): lax.ppermute(head, axis, [((i + 1) % count, i) for i in range(count)])]
    slice x17 -> x0, local copies, waits for them, and re-layouts: 9.48 us -> none  [the longest x7 6.39 us: with_halo(): head = lax.slice_in_dim(cells, 0, width, axis=dim)]
    ppermute x12 -> x0, waiting for transfers between devices: 9.47 us -> none  [the longest x6 9.46 us: with_halo(): lax.ppermute(tail, axis, [(i, (i + 1) % count) for i in range(count)])]
    ppermute x6 -> x0, local copies, waits for them, and re-layouts: 5.98 us -> none  [the longest x3 3.02 us: with_halo(): lax.ppermute(head, axis, [((i + 1) % count, i) for i in range(count)])]
    unnamed x56 -> x0, other arithmetic: 3.93 us -> none
    unnamed x27 -> x6, local copies, waits for them, and re-layouts: 6.9 us -> 3.8 us
  transfers between devices with their start and end apart: 12 -> 0, of which waited for: 3 -> 0; matrix products, arithmetic and copies ran while one was open for 10% -> 0% of each run, Pallas kernels for 0% -> 0%
where the time goes in v1:
time: 25.5 us; the launch traced here: 25.3 us
  Pallas kernels  20.2 us (79%)
  local copies, waits for them, and re-layouts  3.8 us (15%)
  between operations  1.29 us (5%)
    pallas_call x1, Pallas kernels, local(): pl.pallas_call(functools.partial(kernel, sizes), out_shape=(jax.ShapeDtyp...  20.2 us
    unnamed x6, local copies, waits for them, and re-layouts  3.8 us

profile of v1, /device:TPU:0, one launch (start us, length us, event | category | flops | bytes accessed | tf_op | source)
XLA Modules:
  0.0 25.3 jit_solution(1424425183331455678)
XLA Ops:
  1.3 0.0 copy-start
  1.3 1.1 %copy-done = f32[19,4,16,128]{3,2,1,0:T(8,128)S(1)} copy-done((f32[19,4,16,128]{3,2,1,0:T(8,128)S(1)}, f32[19,4,16,128]{3,2,1,0:T(8,128)}, u32[]{:S(2)}) %copy-start) | copy-done | bytes 622616
  2.4 0.0 copy-start.1
  2.4 1.1 %copy-done.1 = f32[19,4,16,128]{3,2,1,0:T(8,128)S(1)} copy-done((f32[19,4,16,128]{3,2,1,0:T(8,128)S(1)}, f32[19,4,16,128]{3,2,1,0:T(8,128)}, u32[]{:S(2)}) %copy-start.1) | copy-done | bytes 622616
  3.4 20.2 %shard_map.50 = (f32[19,4,16,128]{3,2,1,0:T(8,128)S(1)}, f32[19,4,16,128]{3,2,1,0:T(8,128)S(1)}) custom-call(s32[1]{0:T(128)S(6)} %copy.7.shift_ref, f32[19,4,16,128]{3,2,1,0:T(8,128)S(1)} %copy-done, f32[19,4,16,128]{3,2,1,0:T(8,128)S(1)} %copy-done.1), custom_call_target="tpu_custom_call" | custom-call | tf_op jit(solution)/shard_map/pallas_call | solution.py:388
  23.6 0.8 %copy.8 = f32[19,4,16,128]{3,2,1,0:T(8,128)} copy(f32[19,4,16,128]{3,2,1,0:T(8,128)S(1)} %get-tuple-element.4) | data formatting | bytes 1245184
  24.5 0.8 %copy.9 = f32[19,4,16,128]{3,2,1,0:T(8,128)} copy(f32[19,4,16,128]{3,2,1,0:T(8,128)S(1)} %get-tuple-element.5) | data formatting | bytes 1245184
Async XLA Ops:
  1.3 1.1 %copy-start = (f32[19,4,16,128]{3,2,1,0:T(8,128)S(1)}, f32[19,4,16,128]{3,2,1,0:T(8,128)}, u32[]{:S(2)}) copy-start(f32[19,4,16,128]{3,2,1,0:T(8,128)} %f_hbm.1) | copy-start | bytes 1867780
  2.4 1.1 %copy-start.1 = (f32[19,4,16,128]{3,2,1,0:T(8,128)S(1)}, f32[19,4,16,128]{3,2,1,0:T(8,128)}, u32[]{:S(2)}) copy-start(f32[19,4,16,128]{3,2,1,0:T(8,128)} %g_hbm.1) | copy-start | bytes 1867780

commit v2 on v1

--- a/solution.py
+++ b/solution.py
@@ -56,7 +56,6 @@
     phi_yr,
     phi_lo,
     phi_hi,
-    q_ref,
     z_send,
     z_recv,
     up_send,
@@ -75,6 +74,7 @@
     planes, rows, lanes = f_ref.shape[1:]
     a, b, c = lax.axis_index("gx"), lax.axis_index("gy"), lax.axis_index("gz")
     half = count_y // 2
+    outs = (f_out, g_out)
 
     def at(dx, dy, dz=0):
         return (
@@ -227,7 +227,7 @@
 
     def inner(x, carry):
         def put(field, number, value):
-            q_ref[field * POPS + number, x + VELOCITIES[number][0]] = value
+            outs[field][number, x + VELOCITIES[number][0]] = value
 
         collide(x, put)
         return carry
@@ -240,13 +240,13 @@
         if VELOCITIES[number][0] == 1:
             up_send[UP.index((field, number))] = value
         else:
-            q_ref[field * POPS + number, planes - 1 + VELOCITIES[number][0]] = value
+            outs[field][number, planes - 1 + VELOCITIES[number][0]] = value
 
     def put_bottom(field, number, value):
         if VELOCITIES[number][0] == -1:
             down_send[DOWN.index((field, number))] = value
         else:
-            q_ref[field * POPS + number, VELOCITIES[number][0]] = value
+            outs[field][number, VELOCITIES[number][0]] = value
 
     for copy in slides:
         copy.wait()
@@ -300,8 +300,9 @@
             for number in pair:
                 step = VELOCITIES[number][0]
                 for x in range(max(0, -step), planes - max(0, step)):
-                    index = field * POPS + number
-                    q_ref[index, x + step] = along_z(x, k, field, number, q_ref[index, x + step])
+                    outs[field][number, x + step] = along_z(
+                        x, k, field, number, outs[field][number, x + step]
+                    )
 
     def stays(number):
         step = VELOCITIES[number][0]
@@ -312,8 +313,8 @@
             for side, numbers, edge in ((0, Y_UP, rows - 1), (1, Y_DOWN, 0)):
                 for x in stays(numbers[k]):
                     spot = (field * 5 + k) * planes + x
-                    y_send[side, spot : spot + 1, :] = q_ref[
-                        field * POPS + numbers[k], x, edge : edge + 1, :
+                    y_send[side, spot : spot + 1, :] = outs[field][
+                        numbers[k], x, edge : edge + 1, :
                     ]
     y_up = send(y_send.at[0], y_recv.at[0], y_next)
     y_down = send(y_send.at[1], y_recv.at[1], y_prev)
@@ -323,46 +324,27 @@
         for k in range(5):
             for x in stays(Y_UP[k]):
                 spot = (field * 5 + k) * planes + x
-                index = field * POPS + Y_UP[k]
-                q_ref[index, x] = jnp.where(
-                    row_first, y_recv[0, spot : spot + 1, :], pltpu.roll(q_ref[index, x], 1, 0)
+                index = Y_UP[k]
+                outs[field][index, x] = jnp.where(
+                    row_first, y_recv[0, spot : spot + 1, :], pltpu.roll(outs[field][index, x], 1, 0)
                 )
             for x in stays(Y_DOWN[k]):
                 spot = (field * 5 + k) * planes + x
-                index = field * POPS + Y_DOWN[k]
-                q_ref[index, x] = jnp.where(
+                index = Y_DOWN[k]
+                outs[field][index, x] = jnp.where(
                     row_last,
                     y_recv[1, spot : spot + 1, :],
-                    pltpu.roll(q_ref[index, x], rows - 1, 0),
+                    pltpu.roll(outs[field][index, x], rows - 1, 0),
                 )
-
-    stores = []
-
-    def store(field, pops, span):
-        out = (f_out, g_out)[field]
-        lo, hi = pops
-        copy = pltpu.make_async_copy(
-            q_ref.at[pl.ds(field * POPS + lo, hi - lo), span],
-            out.at[pl.ds(lo, hi - lo), span],
-            local_sem.at[2 + len(stores)],
-        )
-        copy.start()
-        stores.append(copy)
-
-    for field in range(2):
-        store(field, (0, 1), pl.ds(0, planes))
-        store(field, (1, 6), pl.ds(1, planes - 1))
-        store(field, (6, 11), pl.ds(0, planes - 1))
-        store(field, (11, POPS), pl.ds(0, planes))
 
     def land(offset, lo_recv, hi_recv):
         for slot in range(lo_recv.shape[0]):
             field, number = UP[offset + slot]
             begin = start_lo - VELOCITIES[number][1]
-            q_ref[field * POPS + number, 0] = lo_recv[slot, pl.ds(begin, rows), :]
+            outs[field][number, 0] = lo_recv[slot, pl.ds(begin, rows), :]
             field, number = DOWN[offset + slot]
             begin = start_hi - VELOCITIES[number][1]
-            q_ref[field * POPS + number, planes - 1] = hi_recv[slot, pl.ds(begin, rows), :]
+            outs[field][number, planes - 1] = hi_recv[slot, pl.ds(begin, rows), :]
 
     for copy in first_up + first_down:
         copy.wait()
@@ -370,12 +352,19 @@
     for copy in second_up + second_down:
         copy.wait()
     land(FIRST, lo_two, hi_two)
-    for field in range(2):
-        store(field, (1, 6), pl.ds(0, 1))
-        store(field, (6, 11), pl.ds(planes - 1, 1))
     for copy in (to_z, to_up, to_down, z_mid, z_top, z_bottom, y_up, y_down):
         copy.wait_send()
-    for copy in stores:
+
+
+def finish(f_in, g_in, f_out, g_out, sem):
+    half = f_in.shape[0] // 2 + 1
+    copies = []
+    for k, (src, dst) in enumerate(((f_in, f_out), (g_in, g_out))):
+        for h, span in enumerate((pl.ds(0, half), pl.ds(half, src.shape[0] - half))):
+            copy = pltpu.make_async_copy(src.at[span], dst.at[span], sem.at[2 * k + h])
+            copy.start()
+            copies.append(copy)
+    for copy in copies:
         copy.wait()
 
 
@@ -385,7 +374,7 @@
     f32 = jnp.float32
     crossing = len(UP)
     copies = 20
-    return pl.pallas_call(
+    f_post, g_post = pl.pallas_call(
         functools.partial(kernel, sizes),
         out_shape=(
             jax.ShapeDtypeStruct(f_pop.shape, f32),
@@ -396,7 +385,7 @@
             pl.BlockSpec(memory_space=pl.ANY),
             pl.BlockSpec(memory_space=pl.ANY),
         ],
-        out_specs=[pl.BlockSpec(memory_space=pl.ANY)] * 2,
+        out_specs=[pl.BlockSpec(memory_space=pltpu.VMEM)] * 2,
         scratch_shapes=[
             pltpu.VMEM(f_pop.shape, f32),
             pltpu.VMEM(g_pop.shape, f32),
@@ -406,7 +395,6 @@
             pltpu.VMEM((2, planes, lanes), f32),
             pltpu.VMEM((2 * rows, lanes), f32),
             pltpu.VMEM((2 * rows, lanes), f32),
-            pltpu.VMEM((2 * POPS, planes) + block, f32),
             pltpu.VMEM((planes, 10) + block, f32),
             pltpu.VMEM((planes, 10) + block, f32),
             pltpu.VMEM((crossing,) + block, f32),
@@ -417,14 +405,25 @@
             pltpu.VMEM((crossing - FIRST, 2 * rows, lanes), f32),
             pltpu.VMEM((2, 10 * planes, lanes), f32),
             pltpu.VMEM((2, 10 * planes, lanes), f32),
-            pltpu.SemaphoreType.DMA((14,)),
+            pltpu.SemaphoreType.DMA((2,)),
             pltpu.SemaphoreType.DMA((copies,)),
             pltpu.SemaphoreType.DMA((copies,)),
         ],
         compiler_params=pltpu.CompilerParams(
-            collective_id=0, has_side_effects=True, vmem_limit_bytes=24 * 1024 * 1024
+            collective_id=0, has_side_effects=True, vmem_limit_bytes=53760 * 1024
         ),
     )(displacement, f_pop, g_pop)
+    return pl.pallas_call(
+        finish,
+        out_shape=(
+            jax.ShapeDtypeStruct(f_pop.shape, f32),
+            jax.ShapeDtypeStruct(g_pop.shape, f32),
+        ),
+        in_specs=[pl.BlockSpec(memory_space=pl.ANY)] * 2,
+        out_specs=[pl.BlockSpec(memory_space=pl.ANY)] * 2,
+        scratch_shapes=[pltpu.SemaphoreType.DMA((4,))],
+        compiler_params=pltpu.CompilerParams(vmem_limit_bytes=53760 * 1024),
+    )(f_post, g_post)
 
 
 def solution(mesh):

time: 25.5 us -> 22.2 us (0.87)
  local copies, waits for them, and re-layouts: 3.8 us -> 0 us
  Pallas kernels: 20.2 us -> 20.8 us
    unnamed x6 -> x0, local copies, waits for them, and re-layouts: 3.8 us -> none
    pallas_call x0 -> x1, Pallas kernels: none -> 1.06 us  [local(): pl.pallas_call(finish, out_shape=(jax.ShapeDtypeStruct(f_pop.shape, f32),...]
    pallas_call x1, Pallas kernels: 20.2 us -> 19.7 us  [local(): pl.pallas_call(functools.partial(kernel, sizes), out_shape=(jax.ShapeDtyp...]
where the time goes in v2:
time: 22.2 us; the launch traced here: 22.1 us
  Pallas kernels  20.8 us (94%)
  between operations  1.28 us (6%)
    pallas_call x1, Pallas kernels, local(): pl.pallas_call(functools.partial(kernel, sizes), out_shape=(jax.ShapeDtyp...  19.7 us
    pallas_call x1, Pallas kernels, local(): pl.pallas_call(finish, out_shape=(jax.ShapeDtypeStruct(f_pop.shape, f32),...  1.06 us

profile of v2, /device:TPU:0, one launch (start us, length us, event | category | flops | bytes accessed | tf_op | source)
XLA Modules:
  0.0 22.1 jit_solution(5889136660694854858)
XLA Ops:
  1.3 19.7 %shard_map.50 = (f32[19,4,16,128]{3,2,1,0:T(8,128)S(1)}, f32[19,4,16,128]{3,2,1,0:T(8,128)S(1)}) custom-call(s32[1]{0:T(128)S(6)} %copy.5.shift_ref, f32[19,4,16,128]{3,2,1,0:T(8,128)} %f_hbm.1, f32[19,4,16,128]{3,2,1,0:T(8,128)} %g_hbm.1), custom_call_target="tpu_custom_call" | custom-call | tf_op jit(solution)/shard_map/pallas_call | solution.py:377
  21.0 1.1 %shard_map.51 = (f32[19,4,16,128]{3,2,1,0:T(8,128)}, f32[19,4,16,128]{3,2,1,0:T(8,128)}) custom-call(f32[19,4,16,128]{3,2,1,0:T(8,128)S(1)} %get-tuple-element.4.f_in, f32[19,4,16,128]{3,2,1,0:T(8,128)S(1)} %get-tuple-element.5.g_in), custom_call_target="tpu_custom_call" | custom-call | tf_op jit(solution)/shard_map/pallas_call | solution.py:416

commit v3 on v2

--- a/solution.py
+++ b/solution.py
@@ -87,14 +87,24 @@
     prev_near, prev_far = at(-1, -half), at(-1, -half - 1)
     y_next, y_prev, z_other = at(0, 1), at(0, -1), at(0, 0, 1)
 
-    load_g = pltpu.make_async_copy(g_hbm, g_ref, local_sem.at[0])
-    load_f = pltpu.make_async_copy(f_hbm, f_ref, local_sem.at[1])
-    load_g.start()
-    load_f.start()
     barrier = pltpu.get_barrier_semaphore()
     partners = (next_near, next_far, prev_near, prev_far, y_next, y_prev, z_other)
     for partner in partners:
         pl.semaphore_signal(barrier, inc=1, device_id=partner, device_id_type=MESH)
+
+    def load(src, dst, parts, base):
+        size = -(-POPS // parts)
+        copies = []
+        for k in range(parts):
+            span = pl.ds(k * size, min(size, POPS - k * size))
+            copies.append(
+                pltpu.make_async_copy(src.at[span], dst.at[span], local_sem.at[base + k])
+            )
+            copies[-1].start()
+        return copies
+
+    load_g = load(g_hbm, g_ref, 4, 0)
+    load_f = load(f_hbm, f_ref, 2, 4)
 
     used = [0]
 
@@ -112,7 +122,8 @@
         copy.start()
         return copy
 
-    load_g.wait()
+    for copy in load_g:
+        copy.wait()
     for x in range(planes):
         parts = [g_ref[i, x] for i in range(POPS)]
         while len(parts) > 1:
@@ -223,7 +234,8 @@
     to_z.wait_recv()
     to_up.wait_recv()
     to_down.wait_recv()
-    load_f.wait()
+    for copy in load_f:
+        copy.wait()
 
     def inner(x, carry):
         def put(field, number, value):
@@ -269,11 +281,11 @@
         ]
 
     collide(planes - 1, put_top)
+    z_top = send(z_send.at[planes - 1], z_recv.at[planes - 1], z_other)
     first_up = send_up(part_one, lo_one)
-    z_top = send(z_send.at[planes - 1], z_recv.at[planes - 1], z_other)
     collide(0, put_bottom)
+    z_bottom = send(z_send.at[0], z_recv.at[0], z_other)
     first_down = send_down(part_one, hi_one)
-    z_bottom = send(z_send.at[0], z_recv.at[0], z_other)
 
     def along_z(x, k, field, number, value):
         plane = z_recv[x, field * 5 + k]
@@ -405,7 +417,7 @@
             pltpu.VMEM((crossing - FIRST, 2 * rows, lanes), f32),
             pltpu.VMEM((2, 10 * planes, lanes), f32),
             pltpu.VMEM((2, 10 * planes, lanes), f32),
-            pltpu.SemaphoreType.DMA((2,)),
+            pltpu.SemaphoreType.DMA((6,)),
             pltpu.SemaphoreType.DMA((copies,)),
             pltpu.SemaphoreType.DMA((copies,)),
         ],

time: 22.2 us -> 22.3 us (level)
  no operation moved by 1% of the time
where the time goes in v3:
time: 22.3 us; the launch traced here: 22.1 us
  Pallas kernels  20.8 us (93%)
  between operations  1.28 us (6%)
    pallas_call x1, Pallas kernels, local(): pl.pallas_call(functools.partial(kernel, sizes), out_shape=(jax.ShapeDtyp...  19.8 us
    pallas_call x1, Pallas kernels, local(): pl.pallas_call(finish, out_shape=(jax.ShapeDtypeStruct(f_pop.shape, f32),...  1.06 us

profile of v3, /device:TPU:0, one launch (start us, length us, event | category | flops | bytes accessed | tf_op | source)
XLA Modules:
  0.0 22.1 jit_solution(2757291752002958535)
XLA Ops:
  1.3 19.8 %shard_map.50 = (f32[19,4,16,128]{3,2,1,0:T(8,128)S(1)}, f32[19,4,16,128]{3,2,1,0:T(8,128)S(1)}) custom-call(s32[1]{0:T(128)S(6)} %copy.5.shift_ref, f32[19,4,16,128]{3,2,1,0:T(8,128)} %f_hbm.1, f32[19,4,16,128]{3,2,1,0:T(8,128)} %g_hbm.1), custom_call_target="tpu_custom_call" | custom-call | tf_op jit(solution)/shard_map/pallas_call | solution.py:389
  21.1 1.1 %shard_map.51 = (f32[19,4,16,128]{3,2,1,0:T(8,128)}, f32[19,4,16,128]{3,2,1,0:T(8,128)}) custom-call(f32[19,4,16,128]{3,2,1,0:T(8,128)S(1)} %get-tuple-element.4.f_in, f32[19,4,16,128]{3,2,1,0:T(8,128)S(1)} %get-tuple-element.5.g_in), custom_call_target="tpu_custom_call" | custom-call | tf_op jit(solution)/shard_map/pallas_call | solution.py:428

commit v4 on v2

--- a/solution.py
+++ b/solution.py
@@ -269,10 +269,14 @@
         ]
 
     collide(planes - 1, put_top)
-    first_up = send_up(part_one, lo_one)
     z_top = send(z_send.at[planes - 1], z_recv.at[planes - 1], z_other)
     collide(0, put_bottom)
-    first_down = send_down(part_one, hi_one)
+    first = [
+        send(up_send.at[part_one], lo_one.at[:, high], next_near),
+        send(down_send.at[part_one], hi_one.at[:, low], prev_near),
+        send(up_send.at[part_one], lo_one.at[:, low], next_far),
+        send(down_send.at[part_one], hi_one.at[:, high], prev_far),
+    ]
     z_bottom = send(z_send.at[0], z_recv.at[0], z_other)
 
     def along_z(x, k, field, number, value):
@@ -346,7 +350,7 @@
             begin = start_hi - VELOCITIES[number][1]
             outs[field][number, planes - 1] = hi_recv[slot, pl.ds(begin, rows), :]
 
-    for copy in first_up + first_down:
+    for copy in first:
         copy.wait()
     land(0, lo_one, hi_one)
     for copy in second_up + second_down:

time: 22.2 us -> 22.3 us (level)
  no operation moved by 1% of the time
where the time goes in v4:
time: 22.3 us; the launch traced here: 22.2 us
  Pallas kernels  20.9 us (94%)
  between operations  1.28 us (6%)
    pallas_call x1, Pallas kernels, local(): pl.pallas_call(functools.partial(kernel, sizes), out_shape=(jax.ShapeDtyp...  19.8 us
    pallas_call x1, Pallas kernels, local(): pl.pallas_call(finish, out_shape=(jax.ShapeDtypeStruct(f_pop.shape, f32),...  1.06 us

profile of v4, /device:TPU:0, one launch (start us, length us, event | category | flops | bytes accessed | tf_op | source)
XLA Modules:
  0.0 22.2 jit_solution(12195325394211772825)
XLA Ops:
  1.3 19.8 %shard_map.50 = (f32[19,4,16,128]{3,2,1,0:T(8,128)S(1)}, f32[19,4,16,128]{3,2,1,0:T(8,128)S(1)}) custom-call(s32[1]{0:T(128)S(6)} %copy.5.shift_ref, f32[19,4,16,128]{3,2,1,0:T(8,128)} %f_hbm.1, f32[19,4,16,128]{3,2,1,0:T(8,128)} %g_hbm.1), custom_call_target="tpu_custom_call" | custom-call | tf_op jit(solution)/shard_map/pallas_call | solution.py:381
  21.1 1.1 %shard_map.51 = (f32[19,4,16,128]{3,2,1,0:T(8,128)}, f32[19,4,16,128]{3,2,1,0:T(8,128)}) custom-call(f32[19,4,16,128]{3,2,1,0:T(8,128)S(1)} %get-tuple-element.4.f_in, f32[19,4,16,128]{3,2,1,0:T(8,128)S(1)} %get-tuple-element.5.g_in), custom_call_target="tpu_custom_call" | custom-call | tf_op jit(solution)/shard_map/pallas_call | solution.py:420
